TPU v7x, 128 devices: a whole 4x4x4 slice. The times are simulated.
128 devices in a mesh: ctx: 64 (over z, x, y), tp: 2 (over core).
Axes of the slice: x: 4, y: 4, z: 4, core: 2. Of those that a mesh axis runs over, the one named last changes fastest.
Arguments:
- streams: bfloat16 [32768, 3, 2048], P('ctx', None, 'tp'), may hold values from -6 to 6
- short_filter: float32 [3, 3, 2048], P(None, None, 'tp'), may hold values from -3.5 to 3.5
- long_filter: float32 [32768, 2048], P('ctx', 'tp'), may hold values from -0.03125 to 0.03125
- skip_gain: float32 [2048], P('tp'), may hold values from -4 to 4
- out_weight: bfloat16 [2048, 4096], P('tp'), may hold values from -0.125 to 0.125
Outputs:
- layer_out: bfloat16 [32768, 4096], P('ctx', 'tp')
All inputs are finite; a program needn't handle non-finite values.
Results may differ from a plain program's by a relative error of at most 0.0049.
Values may be sent and summed in bfloat16 or wider, within the bound.
A program may use at most 192 MiB of HBM per device.

v0:
```python
import functools
import itertools
import math

import jax
import jax.numpy as jnp
import ml_dtypes
import numpy as np
from jax import lax
from jax.experimental import pallas as pl
from jax.experimental.pallas import tpu as pltpu
from jax.sharding import PartitionSpec as P

MESH = pl.DeviceIdType.MESH
bf16, f32 = jnp.bfloat16, jnp.float32

PIECES = 2
OWN = 16 // PIECES
PART = 512 // PIECES
LOW = 4 // PIECES
BLOCK = 128 * PIECES
PAIRS = OWN // 2


def split(a):
    high = a.astype(ml_dtypes.bfloat16)
    return high, (a - high.astype(np.float64)).astype(ml_dtypes.bfloat16)


def tables():
    k1 = np.arange(256) + 0.5
    row = np.arange(256)
    angle = 2 * np.pi * np.outer(k1, 4 * (row % 64) + row // 64) / 512
    first = np.concatenate(split(np.concatenate([np.cos(angle), -np.sin(angle)], 0)), 0)
    twist = 2 * np.pi * np.outer(k1, np.arange(128)) / 65536
    twist = np.concatenate([twist, twist], 1)
    inner = 2 * np.pi * (np.outer(np.arange(128), np.arange(128)) % 128) / 128
    c, s = np.cos(inner), np.sin(inner)
    sh, sl = split(np.block([[c, -s], [s, c]]))
    bh, bl = split(np.block([[c, s], [-s, c]]))
    last = np.concatenate(split(np.concatenate([np.cos(angle.T), -np.sin(angle.T)], 1) * (2.0 / 65536)), 0)
    r = np.arange(256)
    swap = np.zeros((256, 256), ml_dtypes.bfloat16)
    swap[r, (r % 16) * 16 + r // 16] = 1
    r = np.arange(BLOCK)
    pick = np.zeros((BLOCK, BLOCK), ml_dtypes.bfloat16)
    pick[r, (r % PIECES) * 128 + r // PIECES] = 1
    return dict(
        first=first,
        tcos=np.cos(twist).astype(np.float32),
        tsin=np.sin(twist).astype(np.float32),
        second=np.concatenate([sh, sh, sl], 0),
        back=np.concatenate([bh, bh, bl], 0),
        last=last,
        swap=swap,
        pick=pick,
        unit=np.eye(PART, dtype=ml_dtypes.bfloat16),
    )


def offsets():
    every = [d for d in itertools.product(range(4), repeat=3) if d != (0, 0, 0)]
    hops = lambda d: sum(min(v, 4 - v) for v in d)
    order = []
    for d in sorted(every, key=lambda d: (-hops(d), (d[0] * 29 + d[1] * 13 + d[2] * 7) % 31)):
        for e in (d, (d[1], d[2], d[0]), (d[2], d[0], d[1])):
            for g in (e, tuple(-v % 4 for v in e)):
                if g not in order:
                    order.append(g)
    return order


def dot(a, b):
    return jnp.dot(a, b, preferred_element_type=f32)


def dot_t(a, b):
    return lax.dot_general(a, b, (((1,), (1,)), ((), ())), preferred_element_type=f32)


def halves(v):
    high = v.astype(bf16)
    return high, (v - high.astype(f32)).astype(bf16)


def at(i, size):
    return pl.ds(pl.multiple_of(i * size, size), size)


def spread(swap, src, base, dst):
    def group(g, carry):
        mixed = dot(swap[...], src[pl.ds(pl.multiple_of(base + g * 256, 256), 256), :]).astype(bf16)
        for c in range(OWN):
            for high in range(PIECES):
                for low in range(LOW):
                    r = c * PIECES + high
                    dst[pl.ds(pl.multiple_of((high * LOW + low) * 64 + g * 16, 16), 16), pl.ds(c * 128, 128)] = mixed[
                        r * 16 : r * 16 + 16, low * 128 : low * 128 + 128
                    ]
        return carry

    lax.fori_loop(0, 4, group, 0)


def gather(swap, src, tmp, dst, base):
    def group(g, carry):
        for c in range(OWN):
            for high in range(PIECES):
                for low in range(LOW):
                    r = c * PIECES + high
                    tmp[pl.ds(r * 16, 16), pl.ds(low * 128, 128)] = src[
                        pl.ds(pl.multiple_of((high * LOW + low) * 64 + g * 16, 16), 16), pl.ds(c * 128, 128)
                    ]
        dst[pl.ds(pl.multiple_of(base + g * 256, 256), 256), :] = dot(swap[...], tmp[...]).astype(bf16)
        return carry

    lax.fori_loop(0, 4, group, 0)


def forward(t, x):
    a = dot(t["first"][...], x)
    re = a[0:256] + a[512:768]
    im = a[256:512] + a[768:1024]
    tc, ts = t["tcos"][...], t["tsin"][...]
    tre = re * tc + im * ts
    tim = im * tc - re * ts
    z = jnp.concatenate(
        [
            jnp.concatenate([tre[:, :128], tim[:, :128]], 1),
            jnp.concatenate([tre[:, 128:], tim[:, 128:]], 1),
        ],
        0,
    )
    zh, zl = halves(z)
    return dot(jnp.concatenate([zh, zl, zh], 1), t["second"][...])


def backward(t, sx, sh):
    xr, xi, hr, hi = sx[:, :128], sx[:, 128:], sh[:, :128], sh[:, 128:]
    yh, yl = halves(jnp.concatenate([xr * hr - xi * hi, xr * hi + xi * hr], 1))
    b = dot(jnp.concatenate([yh, yl, yh], 1), t["back"][...])
    re = jnp.concatenate([b[:256, :128], b[256:, :128]], 1)
    im = jnp.concatenate([b[:256, 128:], b[256:, 128:]], 1)
    tc, ts = t["tcos"][...], t["tsin"][...]
    vh, vl = halves(jnp.concatenate([re * tc - im * ts, im * tc + re * ts], 0))
    o = dot(t["last"][...], vh)
    return (o[:256] + o[256:] + dot(t["last"][:256, :], vl)).astype(bf16)


NAMES = ("first", "tcos", "tsin", "second", "back", "last", "swap", "pick", "unit")


def kernel(*refs):
    n = len(NAMES)
    streams_in, filter_in, weight_in = refs[:3]
    taps, skip = refs[3:5]
    table_in = refs[5 : 5 + n]
    out = refs[5 + n]
    tabs = refs[6 + n : 6 + 2 * n]
    (sv, hv, halo, gate, extra, block, send_h, send_x, send_y, recv_h, recv_x, recv_y) = refs[6 + 2 * n : 18 + 2 * n]
    (xs, spec, ys, tmp, wa, wb, ga, gb, acc) = refs[18 + 2 * n : 27 + 2 * n]
    load_sem, table_sem, link_send, link_recv, pair_send, pair_recv, halo_sem = refs[27 + 2 * n :]
    t = dict(zip(NAMES, tabs))

    me, tp = lax.axis_index("ctx"), lax.axis_index("tp")
    mz, mx, my = me // 16, (me // 4) % 4, me % 4
    order = offsets()

    def peer(d):
        return ((mz + d[0]) % 4) * 16 + ((mx + d[1]) % 4) * 4 + (my + d[2]) % 4

    load_h = pltpu.make_async_copy(filter_in, hv, load_sem.at[0])
    load_s = pltpu.make_async_copy(streams_in, sv, load_sem.at[1])
    load_w = pltpu.make_async_copy(weight_in.at[:, at(tp, 2048)], wa, load_sem.at[2])
    load_t = [pltpu.make_async_copy(a, b, table_sem.at[i]) for i, (a, b) in enumerate(zip(table_in, tabs))]
    load_t[NAMES.index("pick")].start()
    load_h.start()
    load_s.start()

    barrier = pltpu.get_barrier_semaphore()
    for d in order:
        pl.semaphore_signal(barrier, inc=1, device_id=(peer(d), tp), device_id_type=MESH)
    pl.semaphore_signal(barrier, inc=1, device_id=(me, 1 - tp), device_id_type=MESH)

    for i, copy in enumerate(load_t):
        if NAMES[i] != "pick":
            copy.start()
    load_w.start()

    def send(array, src, dst, q):
        for d in order:
            p = peer(d)
            pltpu.make_async_remote_copy(
                src_ref=src.at[pl.ds(pl.multiple_of(q * 1024 + p * 16, 16), 16)],
                dst_ref=dst.at[pl.ds(pl.multiple_of(q * 1024 + me * 16, 16), 16)],
                send_sem=link_send.at[array * PIECES + q],
                recv_sem=link_recv.at[array * PIECES + q],
                device_id=(p, tp),
                device_id_type=MESH,
            ).start()
        mine = pl.ds(pl.multiple_of(q * 1024 + me * 16, 16), 16)
        dst[mine, :] = src[mine, :]

    def arrived(array, buf, q, sem):
        view = buf.at[pl.ds(0, 63 * 16)]
        pltpu.make_async_copy(view, view, sem.at[array * PIECES + q]).wait()

    load_t[NAMES.index("pick")].wait()
    load_h.wait()

    def filter_block(b, carry):
        cols = at(b, 128)
        for part in range(PIECES):
            block[:, pl.ds(part * 128, 128)] = hv[pl.ds(part * PART, PART), cols].astype(bf16)
        send_h[at(b, BLOCK), :] = dot_t(t["pick"][...], block[...]).astype(bf16)
        return carry

    lax.fori_loop(0, 8, filter_block, 0)

    pl.semaphore_wait(barrier, 64)
    after = (me + 1) % 64
    halo_copy = pltpu.make_async_remote_copy(
        src_ref=streams_in.at[:, pl.ds(496, 16), :],
        dst_ref=halo,
        send_sem=halo_sem.at[0],
        recv_sem=halo_sem.at[1],
        device_id=(after, tp),
        device_id_type=MESH,
    )
    halo_copy.start()
    for q in range(PIECES):
        send(0, send_h, recv_h, q)
    weight_copy = pltpu.make_async_remote_copy(
        src_ref=weight_in.at[:, at(1 - tp, 2048)],
        dst_ref=wb,
        send_sem=pair_send.at[PIECES],
        recv_sem=pair_recv.at[PIECES],
        device_id=(me, 1 - tp),
        device_id_type=MESH,
    )
    weight_copy.start()

    load_s.wait()
    halo_copy.wait_recv()

    def product_block(b, carry):
        cols = at(b, 128)
        for r in range(4):
            rows = pl.ds(r * 128, 128)
            sides = []
            for j in range(3):
                if r == 0:
                    before = halo[j, :, cols].astype(f32)
                    before = jnp.where(me > 0, before, jnp.zeros_like(before))
                else:
                    before = sv[j, pl.ds(r * 128 - 16, 16), cols].astype(f32)
                wide = jnp.concatenate([before, sv[j, rows, cols].astype(f32)], 0)
                sides.append(
                    taps[0, pl.ds(j, 1), cols] * wide[16:]
                    + taps[1, pl.ds(j, 1), cols] * pltpu.roll(wide, 1, 0)[16:]
                    + taps[2, pl.ds(j, 1), cols] * pltpu.roll(wide, 2, 0)[16:]
                )
            product = sides[1] * sides[2]
            gate[rows, cols] = sides[0]
            extra[rows, cols] = skip[:, cols] * product
            part = r * 128 // PART
            block[pl.ds(r * 128 - part * PART, 128), pl.ds(part * 128, 128)] = product.astype(bf16)
        send_x[at(b, BLOCK), :] = dot_t(t["pick"][...], block[...]).astype(bf16)
        return carry

    for q in range(PIECES):
        lax.fori_loop(q * (8 // PIECES), (q + 1) * (8 // PIECES), product_block, 0)
        send(1, send_x, recv_x, q)

    for i, copy in enumerate(load_t):
        if NAMES[i] != "pick":
            copy.wait()

    for q in range(PIECES):
        arrived(0, recv_h, q, link_recv)
        spread(t["swap"], recv_h, q * 1024, xs)

        def filter_pair(j, carry):
            spec[q * PAIRS + j] = forward(t, xs[:, at(j, 256)])
            return carry

        lax.fori_loop(0, PAIRS, filter_pair, 0)

    for q in range(PIECES):
        arrived(1, recv_x, q, link_recv)
        spread(t["swap"], recv_x, q * 1024, xs)

        def product_pair(j, carry):
            ys[:, at(j, 256)] = backward(t, forward(t, xs[:, at(j, 256)]), spec[q * PAIRS + j])
            return carry

        lax.fori_loop(0, PAIRS, product_pair, 0)
        gather(t["swap"], ys, tmp, send_y, q * 1024)
        send(2, send_y, recv_y, q)

    load_w.wait()
    width = 1024 // PIECES
    for q in range(PIECES):
        arrived(2, recv_y, q, link_recv)

        def gate_block(b, carry):
            turned = dot_t(t["unit"][...], recv_y[at(b, BLOCK), :]).astype(bf16)
            conv = dot(turned, t["pick"][...])
            for part in range(PIECES):
                rows, cols = pl.ds(part * PART, PART), at(b, 128)
                ga[rows, cols] = (gate[rows, cols] * (conv[:, part * 128 : part * 128 + 128] + extra[rows, cols])).astype(bf16)
            return carry

        lax.fori_loop(q * (8 // PIECES), (q + 1) * (8 // PIECES), gate_block, 0)
        chans = pl.ds(q * width, width)
        pair_copy = pltpu.make_async_remote_copy(
            src_ref=ga.at[:, chans],
            dst_ref=gb.at[:, chans],
            send_sem=pair_send.at[q],
            recv_sem=pair_recv.at[q],
            device_id=(me, 1 - tp),
            device_id_type=MESH,
        )
        pair_copy.start()

        def own_part(i, carry):
            cols = at(i, 256)
            term = dot(ga[:, chans], wa[chans, cols])
            acc[:, cols] = term if q == 0 else acc[:, cols] + term
            return carry

        lax.fori_loop(0, 8, own_part, 0)
        if q == 0:
            weight_copy.wait()
        pair_copy.wait()

        def other_part(i, carry):
            cols = at(i, 256)
            total = acc[:, cols] + dot(gb[:, chans], wb[chans, cols])
            if q == PIECES - 1:
                out[:, cols] = total.astype(bf16)
            else:
                acc[:, cols] = total
            return carry

        lax.fori_loop(0, 8, other_part, 0)

    halo_copy.wait_send()
    for array, buf in ((0, send_h), (1, send_x), (2, send_y)):
        for q in range(PIECES):
            arrived(array, buf, q, link_send)


def body(streams, short_filter, long_filter, skip_gain, out_weight):
    consts = tables()
    consts = [jnp.asarray(consts[name]) for name in NAMES]
    hbm = pl.BlockSpec(memory_space=pl.ANY)
    vmem = pl.BlockSpec(memory_space=pltpu.VMEM)
    links = lambda: pltpu.VMEM((PIECES * 1024, PART), bf16)
    dma = pltpu.SemaphoreType.DMA
    return pl.pallas_call(
        kernel,
        out_shape=jax.ShapeDtypeStruct((512, 2048), bf16),
        in_specs=[hbm, hbm, hbm, vmem, vmem] + [hbm] * len(NAMES),
        out_specs=vmem,
        scratch_shapes=[pltpu.VMEM(c.shape, c.dtype) for c in consts]
        + [
            pltpu.VMEM((3, 512, 1024), bf16),
            pltpu.VMEM((512, 1024), f32),
            pltpu.VMEM((3, 16, 1024), bf16),
            pltpu.VMEM((512, 1024), f32),
            pltpu.VMEM((512, 1024), f32),
            pltpu.VMEM((PART, BLOCK), bf16),
            links(),
            links(),
            links(),
            links(),
            links(),
            links(),
            pltpu.VMEM((256, OWN * 128), bf16),
            pltpu.VMEM((8, 512, 256), f32),
            pltpu.VMEM((256, OWN * 128), bf16),
            pltpu.VMEM((256, LOW * 128), bf16),
            pltpu.VMEM((1024, 2048), bf16),
            pltpu.VMEM((1024, 2048), bf16),
            pltpu.VMEM((512, 1024), bf16),
            pltpu.VMEM((512, 1024), bf16),
            pltpu.VMEM((512, 2048), f32),
            dma((3,)),
            dma((len(NAMES),)),
            dma((3 * PIECES,)),
            dma((3 * PIECES,)),
            dma((PIECES + 1,)),
            dma((PIECES + 1,)),
            dma((2,)),
        ],
        compiler_params=pltpu.CompilerParams(collective_id=0, has_side_effects=True, vmem_limit_bytes=60 << 20),
        name="hyena",
    )(jnp.transpose(streams, (1, 0, 2)), long_filter, out_weight, short_filter, skip_gain[None, :], *consts)


def solution(mesh):
    return jax.shard_map(
        body,
        mesh=mesh,
        in_specs=(
            P("ctx", None, "tp"),
            P(None, None, "tp"),
            P("ctx", "tp"),
            P("tp"),
            P("tp", None),
        ),
        out_specs=P("ctx", "tp"),
        check_vma=False,
    )
```

profile of v0, /device:TPU:32, one launch (start us, length us, event | category | flops | bytes accessed | tf_op | source)
XLA Modules:
  0.0 78.5 jit_solution(9372936352663579604)
XLA Ops:
  0.0 75.3 %hyena.1 = bf16[512,2048]{1,0:T(8,128)(2,1)} custom-call(bf16[3,512,1024]{2,1,0:T(8,128)(2,1)} %bitcast.2, f32[512,1024]{1,0:T(8,128)} %refs_1_.1, bf16[1024,4096]{1,0:T(8,128)(2,1)} %refs_2_.1, f32[3,3,1024]{2,1,0:T(4,128)} %refs_3_.1, f32[1,1024]{1,0:T(1,128)} %bitcast.3, bf16[1024,256]{1,0:T(8,128)(2,1)} %constant.18.clone.refs_5_, ...), custom_call_target="tpu_custom_call" | custom-call | tf_op jit(solution)/shard_map/hyena/pallas_call | solution.py:361
  75.3 3.2 %copy.16 = bf16[512,2048]{1,0:T(8,128)(2,1)} copy(bf16[512,2048]{1,0:T(8,128)(2,1)} %hyena.1) | data formatting | bytes 4194304
where the time goes:
time: 78.6 us; the launch traced here: 78.5 us
  Pallas kernels  75.3 us (96%)
  local copies, waits for them, and re-layouts  3.16 us (4%)
    pallas_call x1, Pallas kernels, body(): pl.pallas_call(kernel, out_shape=jax.ShapeDtypeStruct((512, 2048), bf16),...  75.3 us
    unnamed x1, local copies, waits for them, and re-layouts  3.16 us

commit v1 on v0

--- a/solution.py
+++ b/solution.py
@@ -1,6 +1,6 @@
 import functools
 import itertools
-import math
+import random
 
 import jax
 import jax.numpy as jnp
@@ -14,12 +14,11 @@
 MESH = pl.DeviceIdType.MESH
 bf16, f32 = jnp.bfloat16, jnp.float32
 
-PIECES = 2
+PIECES = 4
 OWN = 16 // PIECES
 PART = 512 // PIECES
-LOW = 4 // PIECES
 BLOCK = 128 * PIECES
-PAIRS = OWN // 2
+WIDTH = 1024 // PIECES
 
 
 def split(a):
@@ -33,7 +32,6 @@
     angle = 2 * np.pi * np.outer(k1, 4 * (row % 64) + row // 64) / 512
     first = np.concatenate(split(np.concatenate([np.cos(angle), -np.sin(angle)], 0)), 0)
     twist = 2 * np.pi * np.outer(k1, np.arange(128)) / 65536
-    twist = np.concatenate([twist, twist], 1)
     inner = 2 * np.pi * (np.outer(np.arange(128), np.arange(128)) % 128) / 128
     c, s = np.cos(inner), np.sin(inner)
     sh, sl = split(np.block([[c, -s], [s, c]]))
@@ -60,9 +58,9 @@
 
 def offsets():
     every = [d for d in itertools.product(range(4), repeat=3) if d != (0, 0, 0)]
-    hops = lambda d: sum(min(v, 4 - v) for v in d)
+    random.Random(1).shuffle(every)
     order = []
-    for d in sorted(every, key=lambda d: (-hops(d), (d[0] * 29 + d[1] * 13 + d[2] * 7) % 31)):
+    for d in sorted(every, key=lambda d: -sum(min(v, 4 - v) for v in d)):
         for e in (d, (d[1], d[2], d[0]), (d[2], d[0], d[1])):
             for g in (e, tuple(-v % 4 for v in e)):
                 if g not in order:
@@ -87,34 +85,31 @@
     return pl.ds(pl.multiple_of(i * size, size), size)
 
 
-def spread(swap, src, base, dst):
-    def group(g, carry):
-        mixed = dot(swap[...], src[pl.ds(pl.multiple_of(base + g * 256, 256), 256), :]).astype(bf16)
-        for c in range(OWN):
-            for high in range(PIECES):
-                for low in range(LOW):
-                    r = c * PIECES + high
-                    dst[pl.ds(pl.multiple_of((high * LOW + low) * 64 + g * 16, 16), 16), pl.ds(c * 128, 128)] = mixed[
-                        r * 16 : r * 16 + 16, low * 128 : low * 128 + 128
-                    ]
-        return carry
-
-    lax.fori_loop(0, 4, group, 0)
-
-
-def gather(swap, src, tmp, dst, base):
-    def group(g, carry):
-        for c in range(OWN):
-            for high in range(PIECES):
-                for low in range(LOW):
-                    r = c * PIECES + high
-                    tmp[pl.ds(r * 16, 16), pl.ds(low * 128, 128)] = src[
-                        pl.ds(pl.multiple_of((high * LOW + low) * 64 + g * 16, 16), 16), pl.ds(c * 128, 128)
-                    ]
-        dst[pl.ds(pl.multiple_of(base + g * 256, 256), 256), :] = dot(swap[...], tmp[...]).astype(bf16)
-        return carry
-
-    lax.fori_loop(0, 4, group, 0)
+def stack(tiles, rows, columns):
+    return jnp.concatenate([jnp.concatenate([tiles(r, c) for r in range(rows)], 0) for c in range(columns)], 1)
+
+
+def spread(swap, src, q):
+    rows = jnp.concatenate([src[pl.ds(pl.multiple_of(q * 1024 + g * 256, 256), 256), :] for g in range(4)], 1)
+    mixed = dot(swap[...], rows).astype(bf16)
+
+    def tile(r, c):
+        part, g = r // 4, r % 4
+        low = (c * PIECES + part) * 16
+        return mixed[low : low + 16, g * 128 : g * 128 + 128]
+
+    return stack(tile, 16, OWN)
+
+
+def gather(swap, y, dst, q):
+    def tile(r, g):
+        c, part = r // PIECES, r % PIECES
+        low = part * 64 + g * 16
+        return y[low : low + 16, c * 128 : c * 128 + 128]
+
+    mixed = dot(swap[...], stack(tile, 16, 4)).astype(bf16)
+    for g in range(4):
+        dst[pl.ds(pl.multiple_of(q * 1024 + g * 256, 256), 256), :] = mixed[:, g * 128 : g * 128 + 128]
 
 
 def forward(t, x):
@@ -122,16 +117,11 @@
     re = a[0:256] + a[512:768]
     im = a[256:512] + a[768:1024]
     tc, ts = t["tcos"][...], t["tsin"][...]
-    tre = re * tc + im * ts
-    tim = im * tc - re * ts
-    z = jnp.concatenate(
-        [
-            jnp.concatenate([tre[:, :128], tim[:, :128]], 1),
-            jnp.concatenate([tre[:, 128:], tim[:, 128:]], 1),
-        ],
-        0,
-    )
-    zh, zl = halves(z)
+    parts = []
+    for c in range(OWN):
+        r, i = re[:, c * 128 : c * 128 + 128], im[:, c * 128 : c * 128 + 128]
+        parts.append(jnp.concatenate([r * tc + i * ts, i * tc - r * ts], 1))
+    zh, zl = halves(jnp.concatenate(parts, 0))
     return dot(jnp.concatenate([zh, zl, zh], 1), t["second"][...])
 
 
@@ -139,10 +129,13 @@
     xr, xi, hr, hi = sx[:, :128], sx[:, 128:], sh[:, :128], sh[:, 128:]
     yh, yl = halves(jnp.concatenate([xr * hr - xi * hi, xr * hi + xi * hr], 1))
     b = dot(jnp.concatenate([yh, yl, yh], 1), t["back"][...])
-    re = jnp.concatenate([b[:256, :128], b[256:, :128]], 1)
-    im = jnp.concatenate([b[:256, 128:], b[256:, 128:]], 1)
     tc, ts = t["tcos"][...], t["tsin"][...]
-    vh, vl = halves(jnp.concatenate([re * tc - im * ts, im * tc + re * ts], 0))
+    res, ims = [], []
+    for c in range(OWN):
+        r, i = b[c * 256 : c * 256 + 256, :128], b[c * 256 : c * 256 + 256, 128:]
+        res.append(r * tc - i * ts)
+        ims.append(i * tc + r * ts)
+    vh, vl = halves(jnp.concatenate([jnp.concatenate(res, 1), jnp.concatenate(ims, 1)], 0))
     o = dot(t["last"][...], vh)
     return (o[:256] + o[256:] + dot(t["last"][:256, :], vl)).astype(bf16)
 
@@ -158,8 +151,8 @@
     out = refs[5 + n]
     tabs = refs[6 + n : 6 + 2 * n]
     (sv, hv, halo, gate, extra, block, send_h, send_x, send_y, recv_h, recv_x, recv_y) = refs[6 + 2 * n : 18 + 2 * n]
-    (xs, spec, ys, tmp, wa, wb, ga, gb, acc) = refs[18 + 2 * n : 27 + 2 * n]
-    load_sem, table_sem, link_send, link_recv, pair_send, pair_recv, halo_sem = refs[27 + 2 * n :]
+    (spec, wa, wb, ga, gb, acc, done) = refs[18 + 2 * n : 25 + 2 * n]
+    load_sem, table_sem, link_send, link_recv, pair_send, pair_recv, halo_sem, out_sem = refs[25 + 2 * n :]
     t = dict(zip(NAMES, tabs))
 
     me, tp = lax.axis_index("ctx"), lax.axis_index("tp")
@@ -228,8 +221,12 @@
         device_id_type=MESH,
     )
     halo_copy.start()
-    for q in range(PIECES):
+
+    def send_filter(q, carry):
         send(0, send_h, recv_h, q)
+        return carry
+
+    lax.fori_loop(0, PIECES, send_filter, 0)
     weight_copy = pltpu.make_async_remote_copy(
         src_ref=weight_in.at[:, at(1 - tp, 2048)],
         dst_ref=wb,
@@ -268,38 +265,36 @@
         send_x[at(b, BLOCK), :] = dot_t(t["pick"][...], block[...]).astype(bf16)
         return carry
 
-    for q in range(PIECES):
+    def send_product(q, carry):
         lax.fori_loop(q * (8 // PIECES), (q + 1) * (8 // PIECES), product_block, 0)
         send(1, send_x, recv_x, q)
+        return carry
+
+    lax.fori_loop(0, PIECES, send_product, 0)
 
     for i, copy in enumerate(load_t):
         if NAMES[i] != "pick":
             copy.wait()
 
-    for q in range(PIECES):
+    def filter_piece(q, carry):
         arrived(0, recv_h, q, link_recv)
-        spread(t["swap"], recv_h, q * 1024, xs)
-
-        def filter_pair(j, carry):
-            spec[q * PAIRS + j] = forward(t, xs[:, at(j, 256)])
-            return carry
-
-        lax.fori_loop(0, PAIRS, filter_pair, 0)
-
-    for q in range(PIECES):
+        spec[q] = forward(t, spread(t["swap"], recv_h, q))
+        return carry
+
+    lax.fori_loop(0, PIECES, filter_piece, 0)
+
+    def product_piece(q, carry):
         arrived(1, recv_x, q, link_recv)
-        spread(t["swap"], recv_x, q * 1024, xs)
-
-        def product_pair(j, carry):
-            ys[:, at(j, 256)] = backward(t, forward(t, xs[:, at(j, 256)]), spec[q * PAIRS + j])
-            return carry
-
-        lax.fori_loop(0, PAIRS, product_pair, 0)
-        gather(t["swap"], ys, tmp, send_y, q * 1024)
+        y = backward(t, forward(t, spread(t["swap"], recv_x, q)), spec[q])
+        gather(t["swap"], y, send_y, q)
         send(2, send_y, recv_y, q)
+        return carry
+
+    lax.fori_loop(0, PIECES, product_piece, 0)
 
     load_w.wait()
-    width = 1024 // PIECES
+    weight_copy.wait()
+    copies = []
     for q in range(PIECES):
         arrived(2, recv_y, q, link_recv)
 
@@ -312,43 +307,68 @@
             return carry
 
         lax.fori_loop(q * (8 // PIECES), (q + 1) * (8 // PIECES), gate_block, 0)
-        chans = pl.ds(q * width, width)
-        pair_copy = pltpu.make_async_remote_copy(
-            src_ref=ga.at[:, chans],
-            dst_ref=gb.at[:, chans],
-            send_sem=pair_send.at[q],
-            recv_sem=pair_recv.at[q],
-            device_id=(me, 1 - tp),
-            device_id_type=MESH,
+        chans = pl.ds(q * WIDTH, WIDTH)
+        copies.append(
+            pltpu.make_async_remote_copy(
+                src_ref=ga.at[:, chans],
+                dst_ref=gb.at[:, chans],
+                send_sem=pair_send.at[q],
+                recv_sem=pair_recv.at[q],
+                device_id=(me, 1 - tp),
+                device_id_type=MESH,
+            )
         )
-        pair_copy.start()
-
-        def own_part(i, carry):
+        copies[q].start()
+        if q > 0:
+            copies[q - 1].wait()
+
+        def project(i, carry):
             cols = at(i, 256)
-            term = dot(ga[:, chans], wa[chans, cols])
-            acc[:, cols] = term if q == 0 else acc[:, cols] + term
+            left, right = ga[:, chans], wa[chans, cols]
+            if q == 0:
+                acc[:, cols] = dot(left, right)
+            else:
+                before = pl.ds((q - 1) * WIDTH, WIDTH)
+                left = jnp.concatenate([left, gb[:, before]], 1)
+                right = jnp.concatenate([right, wb[before, cols]], 0)
+                acc[:, cols] = acc[:, cols] + dot(left, right)
             return carry
 
-        lax.fori_loop(0, 8, own_part, 0)
-        if q == 0:
-            weight_copy.wait()
-        pair_copy.wait()
-
-        def other_part(i, carry):
-            cols = at(i, 256)
-            total = acc[:, cols] + dot(gb[:, chans], wb[chans, cols])
-            if q == PIECES - 1:
-                out[:, cols] = total.astype(bf16)
-            else:
-                acc[:, cols] = total
-            return carry
-
-        lax.fori_loop(0, 8, other_part, 0)
-
+        lax.fori_loop(0, 8, project, 0)
+
+    copies[-1].wait()
+
+    def out_copy(i):
+        return pltpu.make_async_copy(done.at[:, at(i, 512)], out.at[:, at(i, 512)], out_sem.at[i])
+
+    def finish(i, carry):
+        for half in range(2):
+            cols = at(2 * i + half, 256)
+            final = pl.ds((PIECES - 1) * WIDTH, WIDTH)
+            done[:, cols] = (acc[:, cols] + dot(gb[:, final], wb[final, cols])).astype(bf16)
+        out_copy(i).start()
+        return carry
+
+    lax.fori_loop(0, 4, finish, 0)
+    for i in range(4):
+        out_copy(i).wait()
     halo_copy.wait_send()
     for array, buf in ((0, send_h), (1, send_x), (2, send_y)):
         for q in range(PIECES):
             arrived(array, buf, q, link_send)
+
+
+def handed_on(src, dst, held, sem):
+    rows = [pl.ds(i * 128, 128) for i in range(4)]
+    reads = [pltpu.make_async_copy(src.at[r], held.at[r], sem.at[0, i]) for i, r in enumerate(rows)]
+    writes = [pltpu.make_async_copy(held.at[r], dst.at[r], sem.at[1, i]) for i, r in enumerate(rows)]
+    for copy in reads:
+        copy.start()
+    for i in range(4):
+        reads[i].wait()
+        writes[i].start()
+    for copy in writes:
+        copy.wait()
 
 
 def body(streams, short_filter, long_filter, skip_gain, out_weight):
@@ -358,11 +378,11 @@
     vmem = pl.BlockSpec(memory_space=pltpu.VMEM)
     links = lambda: pltpu.VMEM((PIECES * 1024, PART), bf16)
     dma = pltpu.SemaphoreType.DMA
-    return pl.pallas_call(
+    result = pl.pallas_call(
         kernel,
         out_shape=jax.ShapeDtypeStruct((512, 2048), bf16),
         in_specs=[hbm, hbm, hbm, vmem, vmem] + [hbm] * len(NAMES),
-        out_specs=vmem,
+        out_specs=hbm,
         scratch_shapes=[pltpu.VMEM(c.shape, c.dtype) for c in consts]
         + [
             pltpu.VMEM((3, 512, 1024), bf16),
@@ -377,15 +397,13 @@
             links(),
             links(),
             links(),
-            pltpu.VMEM((256, OWN * 128), bf16),
-            pltpu.VMEM((8, 512, 256), f32),
-            pltpu.VMEM((256, OWN * 128), bf16),
-            pltpu.VMEM((256, LOW * 128), bf16),
+            pltpu.VMEM((PIECES, OWN * 256, 256), f32),
             pltpu.VMEM((1024, 2048), bf16),
             pltpu.VMEM((1024, 2048), bf16),
             pltpu.VMEM((512, 1024), bf16),
             pltpu.VMEM((512, 1024), bf16),
             pltpu.VMEM((512, 2048), f32),
+            pltpu.VMEM((512, 2048), bf16),
             dma((3,)),
             dma((len(NAMES),)),
             dma((3 * PIECES,)),
@@ -393,10 +411,19 @@
             dma((PIECES + 1,)),
             dma((PIECES + 1,)),
             dma((2,)),
+            dma((4,)),
         ],
         compiler_params=pltpu.CompilerParams(collective_id=0, has_side_effects=True, vmem_limit_bytes=60 << 20),
         name="hyena",
     )(jnp.transpose(streams, (1, 0, 2)), long_filter, out_weight, short_filter, skip_gain[None, :], *consts)
+    return pl.pallas_call(
+        handed_on,
+        out_shape=jax.ShapeDtypeStruct((512, 2048), bf16),
+        in_specs=[hbm],
+        out_specs=hbm,
+        scratch_shapes=[pltpu.VMEM((512, 2048), bf16), dma((2, 4))],
+        name="handed_on",
+    )(result)
 
 
 def solution(mesh):

time: 78.6 us -> 69.1 us (0.88)
  the two profiles are of different devices: /device:TPU:32 before, /device:TPU:1 now
where the time goes in v1:
time: 69.1 us; the launch traced here: 68.3 us
  Pallas kernels  68.3 us (99%)
    pallas_call x1, Pallas kernels, body(): pl.pallas_call(kernel, out_shape=jax.ShapeDtypeStruct((512, 2048), bf16),...  65.9 us
    pallas_call x1, Pallas kernels, body(): pl.pallas_call(handed_on, out_shape=jax.ShapeDtypeStruct((512, 2048), bf1...  2.42 us

profile of v1, /device:TPU:1, one launch (start us, length us, event | category | flops | bytes accessed | tf_op | source)
XLA Modules:
  0.0 68.3 jit_solution(12333293448676704927)
XLA Ops:
  0.0 65.9 %hyena.1.src = bf16[512,2048]{1,0:T(8,128)(2,1)} custom-call(bf16[3,512,1024]{2,1,0:T(8,128)(2,1)} %bitcast.2, f32[512,1024]{1,0:T(8,128)} %refs_1_.1, bf16[1024,4096]{1,0:T(8,128)(2,1)} %refs_2_.1, f32[3,3,1024]{2,1,0:T(4,128)} %refs_3_.1, f32[1,1024]{1,0:T(1,128)} %bitcast.3, bf16[1024,256]{1,0:T(8,128)(2,1)} %constant.18.clone.refs_5_, ...), custom_call_target="tpu_custom_call" | custom-call | tf_op jit(solution)/shard_map/hyena/pallas_call | solution.py:381
  65.9 2.4 %handed_on.1 = bf16[512,2048]{1,0:T(8,128)(2,1)} custom-call(bf16[512,2048]{1,0:T(8,128)(2,1)} %hyena.1.src), custom_call_target="tpu_custom_call" | custom-call | tf_op jit(solution)/shard_map/handed_on/pallas_call | solution.py:419

commit v2 on v1

v2 whole, which is shorter than its diff:
```python
import functools
import itertools
import random

import jax
import jax.numpy as jnp
import ml_dtypes
import numpy as np
from jax import lax
from jax.experimental import pallas as pl
from jax.experimental.pallas import tpu as pltpu
from jax.sharding import PartitionSpec as P

MESH = pl.DeviceIdType.MESH
bf16, f32 = jnp.bfloat16, jnp.float32

PIECES = 4
OWN = 16 // PIECES
PART = 512 // PIECES
BLOCK = 128 * PIECES
WIDTH = 1024 // PIECES
STEPS = (2, 2, 2)


def split(a):
    high = a.astype(ml_dtypes.bfloat16)
    return high, (a - high.astype(np.float64)).astype(ml_dtypes.bfloat16)


def tables():
    k1 = np.arange(256) + 0.5
    row = np.arange(256)
    angle = 2 * np.pi * np.outer(k1, 4 * (row % 64) + row // 64) / 512
    first = np.concatenate(split(np.concatenate([np.cos(angle), -np.sin(angle)], 0)), 0)
    twist = 2 * np.pi * np.outer(k1, np.arange(128)) / 65536
    inner = 2 * np.pi * (np.outer(np.arange(128), np.arange(128)) % 128) / 128
    c, s = np.cos(inner), np.sin(inner)
    sh, sl = split(np.block([[c, -s], [s, c]]))
    bh, bl = split(np.block([[c, s], [-s, c]]))
    last = np.concatenate(split(np.concatenate([np.cos(angle.T), -np.sin(angle.T)], 1) * (2.0 / 65536)), 0)
    r = np.arange(256)
    swap = np.zeros((256, 256), ml_dtypes.bfloat16)
    swap[r, (r % 16) * 16 + r // 16] = 1
    r = np.arange(BLOCK)
    pick = np.zeros((BLOCK, BLOCK), ml_dtypes.bfloat16)
    pick[r, (r % PIECES) * 128 + r // PIECES] = 1
    return dict(
        first=first,
        tcos=np.cos(twist).astype(np.float32),
        tsin=np.sin(twist).astype(np.float32),
        second=np.concatenate([sh, sh, sl], 0),
        back=np.concatenate([bh, bh, bl], 0),
        last=last,
        swap=swap,
        pick=pick,
    )


def offsets():
    every = [d for d in itertools.product(range(4), repeat=3) if d != (0, 0, 0)]
    random.Random(1).shuffle(every)
    order = []
    for d in sorted(every, key=lambda d: -sum(min(v, 4 - v) for v in d)):
        for e in (d, (d[1], d[2], d[0]), (d[2], d[0], d[1])):
            for g in (e, tuple(-v % 4 for v in e)):
                if g not in order:
                    order.append(g)
    return order


def dot(a, b):
    return jnp.dot(a, b, preferred_element_type=f32)


def dot_t(a, b):
    return lax.dot_general(a, b, (((1,), (1,)), ((), ())), preferred_element_type=f32)


def halves(v):
    high = v.astype(bf16)
    return high, (v - high.astype(f32)).astype(bf16)


def at(i, size):
    return pl.ds(pl.multiple_of(i * size, size), size)


def stack(tiles, rows, columns):
    return jnp.concatenate([jnp.concatenate([tiles(r, c) for r in range(rows)], 0) for c in range(columns)], 1)


def place(q, step):
    return (q // step) * 1024, (q % step) * 128


def spread(swap, src, row, lane):
    rows = jnp.concatenate(
        [src[pl.ds(pl.multiple_of(row + g * 256, 256), 256), pl.ds(lane, 128)] for g in range(4)], 1
    )
    mixed = dot(swap[...], rows).astype(bf16)

    def tile(r, c):
        part, g = r // 4, r % 4
        low = (c * PIECES + part) * 16
        return mixed[low : low + 16, g * 128 : g * 128 + 128]

    return stack(tile, 16, OWN)


def gather(swap, y, dst, row, lane):
    def tile(r, g):
        c, part = r // PIECES, r % PIECES
        low = part * 64 + g * 16
        return y[low : low + 16, c * 128 : c * 128 + 128]

    mixed = dot(swap[...], stack(tile, 16, 4)).astype(bf16)
    for g in range(4):
        dst[pl.ds(pl.multiple_of(row + g * 256, 256), 256), pl.ds(lane, 128)] = mixed[:, g * 128 : g * 128 + 128]


def forward(t, x):
    a = dot(t["first"][...], x)
    re = a[0:256] + a[512:768]
    im = a[256:512] + a[768:1024]
    tc, ts = t["tcos"][...], t["tsin"][...]
    parts = []
    for c in range(OWN):
        r, i = re[:, c * 128 : c * 128 + 128], im[:, c * 128 : c * 128 + 128]
        parts.append(jnp.concatenate([r * tc + i * ts, i * tc - r * ts], 1))
    zh, zl = halves(jnp.concatenate(parts, 0))
    return dot(jnp.concatenate([zh, zl, zh], 1), t["second"][...])


def backward(t, sx, sh, count):
    xr, xi, hr, hi = sx[:, :128], sx[:, 128:], sh[:, :128], sh[:, 128:]
    yh, yl = halves(jnp.concatenate([xr * hr - xi * hi, xr * hi + xi * hr], 1))
    b = dot(jnp.concatenate([yh, yl, yh], 1), t["back"][...])
    tc, ts = t["tcos"][...], t["tsin"][...]
    res, ims = [], []
    for c in range(count):
        r, i = b[c * 256 : c * 256 + 256, :128], b[c * 256 : c * 256 + 256, 128:]
        res.append(r * tc - i * ts)
        ims.append(i * tc + r * ts)
    vh, vl = halves(jnp.concatenate([jnp.concatenate(res, 1), jnp.concatenate(ims, 1)], 0))
    o = dot(t["last"][...], vh)
    return (o[:256] + o[256:] + dot(t["last"][:256, :], vl)).astype(bf16)


NAMES = ("first", "tcos", "tsin", "second", "back", "last", "swap", "pick")


def kernel(*refs):
    n = len(NAMES)
    streams_in, filter_in, weight_in = refs[:3]
    taps, skip = refs[3:5]
    table_in = refs[5 : 5 + n]
    out = refs[5 + n]
    tabs = refs[6 + n : 6 + 2 * n]
    (sv, hv, tail, halo, gate, extra, send_h, send_x, send_y, recv_h, recv_x, recv_y) = refs[6 + 2 * n : 18 + 2 * n]
    (xs, sx, ys, spec, wa, wb, ga, gb, acc, done) = refs[18 + 2 * n : 28 + 2 * n]
    load_sem, table_sem, link_send, link_recv, pair_send, pair_recv, halo_sem, out_sem = refs[28 + 2 * n :]
    t = dict(zip(NAMES, tabs))

    me, tp = lax.axis_index("ctx"), lax.axis_index("tp")
    mz, mx, my = me // 16, lax.rem(me // 4, 4), lax.rem(me, 4)
    along = [[lax.rem(m + i, 4) * scale for i in range(4)] for m, scale in ((mz, 16), (mx, 4), (my, 1))]
    order = offsets()

    def peer(d):
        return along[0][d[0]] + along[1][d[1]] + along[2][d[2]]

    load_h = pltpu.make_async_copy(filter_in, hv, load_sem.at[0])
    load_s = pltpu.make_async_copy(streams_in, sv, load_sem.at[1])
    load_w = pltpu.make_async_copy(weight_in.at[:, at(tp, 2048)], wa, load_sem.at[2])
    load_t = [pltpu.make_async_copy(a, b, table_sem.at[i]) for i, (a, b) in enumerate(zip(table_in, tabs))]
    load_t[NAMES.index("pick")].start()
    load_h.start()
    load_s.start()

    barrier = pltpu.get_barrier_semaphore()
    for d in order:
        pl.semaphore_signal(barrier, inc=1, device_id=(peer(d), tp), device_id_type=MESH)
    pl.semaphore_signal(barrier, inc=1, device_id=(me, 1 - tp), device_id_type=MESH)

    for i, copy in enumerate(load_t):
        if NAMES[i] != "pick":
            copy.start()
    load_w.start()

    def send(array, src, dst, q):
        base = (q // STEPS[array]) * 1024
        for d in order:
            p = peer(d)
            pltpu.make_async_remote_copy(
                src_ref=src.at[pl.ds(pl.multiple_of(base + p * 16, 16), 16)],
                dst_ref=dst.at[pl.ds(pl.multiple_of(base + me * 16, 16), 16)],
                send_sem=link_send.at[array * PIECES + q],
                recv_sem=link_recv.at[array * PIECES + q],
                device_id=(p, tp),
                device_id_type=MESH,
            ).start()
        mine = pl.ds(pl.multiple_of(base + me * 16, 16), 16)
        dst[mine, :] = src[mine, :]

    def arrived(array, buf, q, sem):
        view = buf.at[pl.ds(0, 63 * 16)]
        pltpu.make_async_copy(view, view, sem.at[array * PIECES + q]).wait()

    def block_at(array, b):
        row, lane = place(b // 2, STEPS[array])
        return pl.ds(pl.multiple_of(row + (b % 2) * BLOCK, BLOCK), BLOCK), pl.ds(pl.multiple_of(lane, 128), 128)

    load_t[NAMES.index("pick")].wait()
    load_h.wait()

    def filter_block(b, carry):
        parts = [hv[pl.ds(part * PART, PART), at(b, 128)].astype(bf16) for part in range(PIECES)]
        send_h[block_at(0, b)] = dot_t(t["pick"][...], jnp.concatenate(parts, 1)).astype(bf16)
        return carry

    lax.fori_loop(0, 8, filter_block, 0, unroll=4)

    load_s.wait()
    line = lax.broadcasted_iota(jnp.int32, (16, 1024), 0)
    packed = jnp.zeros((16, 1024), f32)
    for j in range(3):
        rows = pltpu.roll(sv[j, pl.ds(496, 16), :].astype(f32), 2 + 2 * j, 0)
        packed = jnp.where((line >= 2 * j) & (line < 2 * j + 2), rows, packed)
    tail[...] = packed.astype(bf16)

    pl.semaphore_wait(barrier, 64)
    after = lax.rem(me + 1, 64)
    for i in range(4):
        pltpu.make_async_remote_copy(
            src_ref=tail.at[:, pl.ds(i * 256, 256)],
            dst_ref=halo.at[:, pl.ds(i * 256, 256)],
            send_sem=halo_sem.at[0],
            recv_sem=halo_sem.at[1],
            device_id=(after, tp),
            device_id_type=MESH,
        ).start()
    for q in range(0, PIECES, STEPS[0]):
        send(0, send_h, recv_h, q)
    pltpu.make_async_copy(halo, halo, halo_sem.at[1]).wait()

    def product_block(b, carry):
        cols = at(b, 128)
        parts = []
        for r in range(4):
            rows = pl.ds(r * 128, 128)
            sides = []
            for j in range(3):
                if r == 0:
                    before = pltpu.roll(halo[:, cols].astype(f32), 14 - 2 * j, 0)
                    before = jnp.where(me > 0, before, jnp.zeros_like(before))
                else:
                    before = sv[j, pl.ds(r * 128 - 16, 16), cols].astype(f32)
                now = sv[j, rows, cols].astype(f32)
                wide = jnp.concatenate([before[8:], now], 0)
                sides.append(
                    taps[0, pl.ds(j, 1), cols] * now
                    + taps[1, pl.ds(j, 1), cols] * pltpu.roll(wide, 1, 0)[8:]
                    + taps[2, pl.ds(j, 1), cols] * pltpu.roll(wide, 2, 0)[8:]
                )
            product = sides[1] * sides[2]
            gate[rows, cols] = sides[0]
            extra[rows, cols] = skip[:, cols] * product
            parts.append(product.astype(bf16))
        send_x[block_at(1, b)] = dot_t(t["pick"][...], jnp.concatenate(parts, 1)).astype(bf16)
        return carry

    for q in range(0, PIECES, STEPS[1]):
        lax.fori_loop(2 * q, 2 * (q + STEPS[1]), product_block, 0, unroll=2)
        send(1, send_x, recv_x, q)

    weight_copy = pltpu.make_async_remote_copy(
        src_ref=weight_in.at[:, at(1 - tp, 2048)],
        dst_ref=wb,
        send_sem=pair_send.at[PIECES],
        recv_sem=pair_recv.at[PIECES],
        device_id=(me, 1 - tp),
        device_id_type=MESH,
    )
    weight_copy.start()

    for i, copy in enumerate(load_t):
        if NAMES[i] != "pick":
            copy.wait()

    for q in range(0, PIECES, STEPS[0]):
        arrived(0, recv_h, q, link_recv)
        for k in range(STEPS[0]):
            xs[k] = spread(t["swap"], recv_h, *place(q + k, STEPS[0]))
        for k in range(STEPS[0]):
            spec[q + k] = forward(t, xs[k])

    for q in range(0, PIECES, STEPS[1]):
        arrived(1, recv_x, q, link_recv)
        for k in range(STEPS[1]):
            xs[k] = spread(t["swap"], recv_x, *place(q + k, STEPS[1]))
        for k in range(STEPS[1]):
            sx[k] = forward(t, xs[k])
        for k in range(STEPS[1]):
            for m in range(2):
                rows = pl.ds(m * 512, 512)
                ys[k, :, pl.ds(m * 256, 256)] = backward(t, sx[k, rows, :], spec[q + k, rows, :], 2)
        for k in range(STEPS[1]):
            gather(t["swap"], ys[k], send_y, *place(q + k, STEPS[2]))
        if STEPS[2] <= STEPS[1]:
            for k in range(0, STEPS[1], STEPS[2]):
                send(2, send_y, recv_y, q + k)

    load_w.wait()
    weight_copy.wait()
    copies = []

    def gate_block(b, carry):
        conv = dot(recv_y[block_at(2, b)].astype(f32).T.astype(bf16), t["pick"][...])
        for part in range(PIECES):
            rows, cols = pl.ds(part * PART, PART), at(b, 128)
            ga[rows, cols] = (gate[rows, cols] * (conv[:, part * 128 : part * 128 + 128] + extra[rows, cols])).astype(bf16)
        return carry

    def gated(q):
        arrived(2, recv_y, q, link_recv)
        lax.fori_loop(2 * q, 2 * (q + STEPS[2]), gate_block, 0, unroll=2)
        chans = pl.ds(q * WIDTH, STEPS[2] * WIDTH)
        copy = pltpu.make_async_remote_copy(
            src_ref=ga.at[:, chans],
            dst_ref=gb.at[:, chans],
            send_sem=pair_send.at[q],
            recv_sem=pair_recv.at[q],
            device_id=(me, 1 - tp),
            device_id_type=MESH,
        )
        copy.start()
        copies.append(copy)

    early = PIECES - STEPS[2]
    for q in range(0, early, STEPS[2]):
        gated(q)
    for copy in copies:
        copy.wait()
    first, final = pl.ds(0, early * WIDTH), pl.ds(early * WIDTH, STEPS[2] * WIDTH)

    def project_first(i, carry):
        cols = at(i, 256)
        left = jnp.concatenate([ga[:, first], gb[:, first]], 1)
        acc[:, cols] = dot(left, jnp.concatenate([wa[first, cols], wb[first, cols]], 0))
        return carry

    lax.fori_loop(0, 8, project_first, 0, unroll=2)
    gated(early)

    def project_own(i, carry):
        cols = at(i, 256)
        acc[:, cols] = acc[:, cols] + dot(ga[:, final], wa[final, cols])
        return carry

    lax.fori_loop(0, 8, project_own, 0, unroll=2)
    copies[-1].wait()

    def out_copy(i):
        return pltpu.make_async_copy(done.at[:, at(i, 512)], out.at[:, at(i, 512)], out_sem.at[i])

    def finish(i, carry):
        for half in range(2):
            cols = at(2 * i + half, 256)
            done[:, cols] = (acc[:, cols] + dot(gb[:, final], wb[final, cols])).astype(bf16)
        out_copy(i).start()
        return carry

    lax.fori_loop(0, 4, finish, 0)
    for i in range(4):
        out_copy(i).wait()
    pltpu.make_async_copy(tail, tail, halo_sem.at[0]).wait()
    for array, buf in ((0, send_h), (1, send_x), (2, send_y)):
        for q in range(0, PIECES, STEPS[array]):
            arrived(array, buf, q, link_send)


def handed_on(src, dst, held, sem):
    rows = [pl.ds(i * 128, 128) for i in range(4)]
    reads = [pltpu.make_async_copy(src.at[r], held.at[r], sem.at[0, i]) for i, r in enumerate(rows)]
    writes = [pltpu.make_async_copy(held.at[r], dst.at[r], sem.at[1, i]) for i, r in enumerate(rows)]
    for copy in reads:
        copy.start()
    for i in range(4):
        reads[i].wait()
        writes[i].start()
    for copy in writes:
        copy.wait()


def body(streams, short_filter, long_filter, skip_gain, out_weight):
    consts = tables()
    consts = [jnp.asarray(consts[name]) for name in NAMES]
    hbm = pl.BlockSpec(memory_space=pl.ANY)
    vmem = pl.BlockSpec(memory_space=pltpu.VMEM)
    links = [pltpu.VMEM((PIECES // step * 1024, step * PART), bf16) for step in STEPS]
    dma = pltpu.SemaphoreType.DMA
    result = pl.pallas_call(
        kernel,
        out_shape=jax.ShapeDtypeStruct((512, 2048), bf16),
        in_specs=[hbm, hbm, hbm, vmem, vmem] + [hbm] * len(NAMES),
        out_specs=hbm,
        scratch_shapes=[pltpu.VMEM(c.shape, c.dtype) for c in consts]
        + [
            pltpu.VMEM((3, 512, 1024), bf16),
            pltpu.VMEM((512, 1024), f32),
            pltpu.VMEM((16, 1024), bf16),
            pltpu.VMEM((16, 1024), bf16),
            pltpu.VMEM((512, 1024), f32),
            pltpu.VMEM((512, 1024), f32),
            *links,
            *links,
            pltpu.VMEM((2, 256, 512), bf16),
            pltpu.VMEM((2, 1024, 256), f32),
            pltpu.VMEM((2, 256, 512), bf16),
            pltpu.VMEM((PIECES, OWN * 256, 256), f32),
            pltpu.VMEM((1024, 2048), bf16),
            pltpu.VMEM((1024, 2048), bf16),
            pltpu.VMEM((512, 1024), bf16),
            pltpu.VMEM((512, 1024), bf16),
            pltpu.VMEM((512, 2048), f32),
            pltpu.VMEM((512, 2048), bf16),
            dma((3,)),
            dma((len(NAMES),)),
            dma((3 * PIECES,)),
            dma((3 * PIECES,)),
            dma((PIECES + 1,)),
            dma((PIECES + 1,)),
            dma((2,)),
            dma((4,)),
        ],
        compiler_params=pltpu.CompilerParams(collective_id=0, has_side_effects=True, vmem_limit_bytes=60 << 20),
        name="hyena",
    )(jnp.transpose(streams, (1, 0, 2)), long_filter, out_weight, short_filter, skip_gain[None, :], *consts)
    return pl.pallas_call(
        handed_on,
        out_shape=jax.ShapeDtypeStruct((512, 2048), bf16),
        in_specs=[hbm],
        out_specs=hbm,
        scratch_shapes=[pltpu.VMEM((512, 2048), bf16), dma((2, 4))],
        name="handed_on",
    )(result)


def solution(mesh):
    return jax.shard_map(
        body,
        mesh=mesh,
        in_specs=(
            P("ctx", None, "tp"),
            P(None, None, "tp"),
            P("ctx", "tp"),
            P("tp"),
            P("tp", None),
        ),
        out_specs=P("ctx", "tp"),
        check_vma=False,
    )
```

time: 69.1 us -> 65.3 us (0.945)
  Pallas kernels: 68.3 us -> 64.9 us
    pallas_call x1, Pallas kernels: 65.9 us -> 62.5 us  [body(): pl.pallas_call(kernel, out_shape=jax.ShapeDtypeStruct((512, 2048), bf16),...]
where the time goes in v2:
time: 65.3 us; the launch traced here: 65.1 us
  Pallas kernels  64.9 us (99%)
    pallas_call x1, Pallas kernels, body(): pl.pallas_call(kernel, out_shape=jax.ShapeDtypeStruct((512, 2048), bf16),...  62.5 us
    pallas_call x1, Pallas kernels, body(): pl.pallas_call(handed_on, out_shape=jax.ShapeDtypeStruct((512, 2048), bf1...  2.42 us

profile of v2, /device:TPU:1, one launch (start us, length us, event | category | flops | bytes accessed | tf_op | source)
XLA Modules:
  0.0 65.1 jit_solution(14868130153245805433)
XLA Ops:
  0.0 62.5 %hyena.1.src = bf16[512,2048]{1,0:T(8,128)(2,1)} custom-call(bf16[3,512,1024]{2,1,0:T(8,128)(2,1)} %bitcast.2, f32[512,1024]{1,0:T(8,128)} %refs_1_.1, bf16[1024,4096]{1,0:T(8,128)(2,1)} %refs_2_.1, f32[3,3,1024]{2,1,0:T(4,128)} %refs_3_.1, f32[1,1024]{1,0:T(1,128)} %bitcast.3, bf16[1024,256]{1,0:T(8,128)(2,1)} %constant.16.clone.refs_5_, ...), custom_call_target="tpu_custom_call" | custom-call | tf_op jit(solution)/shard_map/hyena/pallas_call | solution.py:402
  62.5 2.4 %handed_on.1 = bf16[512,2048]{1,0:T(8,128)(2,1)} custom-call(bf16[512,2048]{1,0:T(8,128)(2,1)} %hyena.1.src), custom_call_target="tpu_custom_call" | custom-call | tf_op jit(solution)/shard_map/handed_on/pallas_call | solution.py:439

commit v3 on v2

--- a/solution.py
+++ b/solution.py
@@ -19,7 +19,7 @@
 PART = 512 // PIECES
 BLOCK = 128 * PIECES
 WIDTH = 1024 // PIECES
-STEPS = (2, 2, 2)
+STEPS = (2, 1, 1)
 
 
 def split(a):
@@ -174,18 +174,18 @@
     load_w = pltpu.make_async_copy(weight_in.at[:, at(tp, 2048)], wa, load_sem.at[2])
     load_t = [pltpu.make_async_copy(a, b, table_sem.at[i]) for i, (a, b) in enumerate(zip(table_in, tabs))]
     load_t[NAMES.index("pick")].start()
-    load_h.start()
-    load_s.start()
+    for i in range(4):
+        part = pl.ds(i * 128, 128)
+        pltpu.make_async_copy(filter_in.at[part], hv.at[part], load_sem.at[0]).start()
+    for i in range(6):
+        part = (i // 2, pl.ds(i % 2 * 256, 256))
+        pltpu.make_async_copy(streams_in.at[part], sv.at[part], load_sem.at[1]).start()
 
     barrier = pltpu.get_barrier_semaphore()
     for d in order:
         pl.semaphore_signal(barrier, inc=1, device_id=(peer(d), tp), device_id_type=MESH)
     pl.semaphore_signal(barrier, inc=1, device_id=(me, 1 - tp), device_id_type=MESH)
 
-    for i, copy in enumerate(load_t):
-        if NAMES[i] != "pick":
-            copy.start()
-    load_w.start()
 
     def send(array, src, dst, q):
         base = (q // STEPS[array]) * 1024
@@ -221,6 +221,10 @@
     lax.fori_loop(0, 8, filter_block, 0, unroll=4)
 
     load_s.wait()
+    for i, copy in enumerate(load_t):
+        if NAMES[i] != "pick":
+            copy.start()
+    load_w.start()
     line = lax.broadcasted_iota(jnp.int32, (16, 1024), 0)
     packed = jnp.zeros((16, 1024), f32)
     for j in range(3):
@@ -385,9 +389,9 @@
     writes = [pltpu.make_async_copy(held.at[r], dst.at[r], sem.at[1, i]) for i, r in enumerate(rows)]
     for copy in reads:
         copy.start()
-    for i in range(4):
-        reads[i].wait()
-        writes[i].start()
+    for read, write in zip(reads, writes):
+        read.wait()
+        write.start()
     for copy in writes:
         copy.wait()
 

time: 65.3 us -> 63.1 us (0.966)
  Pallas kernels: 64.9 us -> 62.8 us
    pallas_call x1, Pallas kernels: 62.5 us -> 60.3 us  [body(): pl.pallas_call(kernel, out_shape=jax.ShapeDtypeStruct((512, 2048), bf16),...]
where the time goes in v3:
time: 63.1 us; the launch traced here: 62.9 us
  Pallas kernels  62.8 us (100%)
    pallas_call x1, Pallas kernels, body(): pl.pallas_call(kernel, out_shape=jax.ShapeDtypeStruct((512, 2048), bf16),...  60.3 us
    pallas_call x1, Pallas kernels, body(): pl.pallas_call(handed_on, out_shape=jax.ShapeDtypeStruct((512, 2048), bf1...  2.42 us

profile of v3, /device:TPU:1, one launch (start us, length us, event | category | flops | bytes accessed | tf_op | source)
XLA Modules:
  0.0 62.9 jit_solution(6329793945488054658)
XLA Ops:
  0.0 60.3 %hyena.1.src = bf16[512,2048]{1,0:T(8,128)(2,1)} custom-call(bf16[3,512,1024]{2,1,0:T(8,128)(2,1)} %bitcast.2, f32[512,1024]{1,0:T(8,128)} %refs_1_.1, bf16[1024,4096]{1,0:T(8,128)(2,1)} %refs_2_.1, f32[3,3,1024]{2,1,0:T(4,128)} %refs_3_.1, f32[1,1024]{1,0:T(1,128)} %bitcast.3, bf16[1024,256]{1,0:T(8,128)(2,1)} %constant.16.clone.refs_5_, ...), custom_call_target="tpu_custom_call" | custom-call | tf_op jit(solution)/shard_map/hyena/pallas_call | solution.py:406
  60.4 2.4 %handed_on.1 = bf16[512,2048]{1,0:T(8,128)(2,1)} custom-call(bf16[512,2048]{1,0:T(8,128)(2,1)} %hyena.1.src), custom_call_target="tpu_custom_call" | custom-call | tf_op jit(solution)/shard_map/handed_on/pallas_call | solution.py:443

commit v4 on v3

--- a/solution.py
+++ b/solution.py
@@ -353,7 +353,7 @@
         acc[:, cols] = dot(left, jnp.concatenate([wa[first, cols], wb[first, cols]], 0))
         return carry
 
-    lax.fori_loop(0, 8, project_first, 0, unroll=2)
+    lax.fori_loop(0, 8, project_first, 0, unroll=4)
     gated(early)
 
     def project_own(i, carry):
@@ -361,7 +361,7 @@
         acc[:, cols] = acc[:, cols] + dot(ga[:, final], wa[final, cols])
         return carry
 
-    lax.fori_loop(0, 8, project_own, 0, unroll=2)
+    lax.fori_loop(0, 8, project_own, 0, unroll=4)
     copies[-1].wait()
 
     def out_copy(i):
@@ -374,7 +374,7 @@
         out_copy(i).start()
         return carry
 
-    lax.fori_loop(0, 4, finish, 0)
+    lax.fori_loop(0, 4, finish, 0, unroll=2)
     for i in range(4):
         out_copy(i).wait()
     pltpu.make_async_copy(tail, tail, halo_sem.at[0]).wait()

time: 63.1 us -> 62.2 us (0.986)
  Pallas kernels: 62.8 us -> 61.8 us
    pallas_call x1, Pallas kernels: 60.3 us -> 59.4 us  [body(): pl.pallas_call(kernel, out_shape=jax.ShapeDtypeStruct((512, 2048), bf16),...]
where the time goes in v4:
time: 62.2 us; the launch traced here: 62 us
  Pallas kernels  61.8 us (99%)
    pallas_call x1, Pallas kernels, body(): pl.pallas_call(kernel, out_shape=jax.ShapeDtypeStruct((512, 2048), bf16),...  59.4 us
    pallas_call x1, Pallas kernels, body(): pl.pallas_call(handed_on, out_shape=jax.ShapeDtypeStruct((512, 2048), bf1...  2.42 us

profile of v4, /device:TPU:1, one launch (start us, length us, event | category | flops | bytes accessed | tf_op | source)
XLA Modules:
  0.0 62.0 jit_solution(18227623849747331440)
XLA Ops:
  0.0 59.4 %hyena.1.src = bf16[512,2048]{1,0:T(8,128)(2,1)} custom-call(bf16[3,512,1024]{2,1,0:T(8,128)(2,1)} %bitcast.2, f32[512,1024]{1,0:T(8,128)} %refs_1_.1, bf16[1024,4096]{1,0:T(8,128)(2,1)} %refs_2_.1, f32[3,3,1024]{2,1,0:T(4,128)} %refs_3_.1, f32[1,1024]{1,0:T(1,128)} %bitcast.3, bf16[1024,256]{1,0:T(8,128)(2,1)} %constant.16.clone.refs_5_, ...), custom_call_target="tpu_custom_call" | custom-call | tf_op jit(solution)/shard_map/hyena/pallas_call | solution.py:406
  59.4 2.4 %handed_on.1 = bf16[512,2048]{1,0:T(8,128)(2,1)} custom-call(bf16[512,2048]{1,0:T(8,128)(2,1)} %hyena.1.src), custom_call_target="tpu_custom_call" | custom-call | tf_op jit(solution)/shard_map/handed_on/pallas_call | solution.py:443
